TPU v7x, 768 devices: a whole 4x8x12 slice. The times are simulated.
768 devices in a mesh: row: 16 (over y, core), col: 48 (over z, x).
Axes of the slice: x: 4, y: 8, z: 12, core: 2. Of those that a mesh axis runs over, the one named last changes fastest.
Arguments:
- three_centre: bfloat16 [64, 2048, 12288], P(None, 'row', 'col'), may hold values from -6 to 6
- block_mask: int32 [1, 32, 192], P(None, 'row', 'col'), may hold values 0 or 1
- g_occ: bfloat16 [12288, 192], P('col'), may hold values from -0.1875 to 0.1875
- g_virt: bfloat16 [2048, 2048], P('row'), may hold values from -0.125 to 0.125
Outputs:
- contracted: bfloat16 [192, 64, 2048], P('col', None, 'row')
All inputs are finite; a program needn't handle non-finite values. No bound on the sum of `block_mask` on one device may be relied on, other than what follows from the above.
Results may differ from a plain program's by a relative error of at most 0.0049.
Values may be sent and summed in bfloat16 or wider, within the bound.
A program may use at most 32 MiB of HBM per device.

v0:
```python
import jax
import jax.numpy as jnp
from jax import lax
from jax.sharding import PartitionSpec as P


def expand_mask(mask_blocks, block_size):
    ri_blocks, mu_blocks, nu_blocks = mask_blocks.shape
    expanded = mask_blocks.astype(jnp.bfloat16)[:, None, :, None, :, None]
    expanded = jnp.broadcast_to(
        expanded, (ri_blocks, block_size, mu_blocks, block_size, nu_blocks, block_size)
    )
    return expanded.reshape(ri_blocks * block_size, mu_blocks * block_size, nu_blocks * block_size)


def shards(three_centre, block_mask, g_occ, g_virt):
    block_size = three_centre.shape[0] // block_mask.shape[0]
    screened = three_centre * expand_mask(block_mask, block_size)
    partial_term = jnp.einsum("pmn,ns->spm", screened, g_occ, preferred_element_type=jnp.float32)
    summed = lax.psum_scatter(partial_term, "col", scatter_dimension=0, tiled=True)
    occupied_half = summed.astype(jnp.bfloat16)
    result = jnp.einsum(
        "spm,lm->spl",
        lax.all_gather(occupied_half, "row", axis=2, tiled=True),
        g_virt,
        preferred_element_type=jnp.float32,
    )
    return result.astype(jnp.bfloat16)


def solution(mesh):
    placed = (P(None, "row", "col"), P(None, "row", "col"), P("col", None), P("row", None))
    return jax.shard_map(
        shards, mesh=mesh, in_specs=placed, out_specs=P("col", None, "row"), check_vma=False
    )
```

profile of v0, /device:TPU:1, one launch (start us, length us, event | category | flops | bytes accessed | tf_op | source)
XLA Modules:
  0.0 519.5 jit_solution(4557414964671012669)
XLA Ops:
  6.5 0.0 copy-start
  6.5 0.0 reduce-scatter.2.cloned.1.call-start
  6.5 0.7 convert_bitcast_fusion
  7.3 0.1 broadcast_in_dim.13
  7.4 0.1 broadcast_in_dim.14
  7.5 3.7 fusion
  11.3 6.3 %copy.7 = f32[64,128,192]{1,0,2:T(8,128)} copy(f32[64,128,192]{1,2,0:T(8,128)S(1)} %fusion) | data formatting | bytes 12582912 | tf_op jit(solution)/shard_map/pmn,ns->spm/dot_general | solution.py:19
  17.6 0.0 reduce-scatter.2.cloned.1.call-update
  17.6 0.0 all-gather.2.cloned.1.call-start
  17.6 442.5 %reduce-scatter.2.cloned.1.call-done = f32[4,64,128]{2,1,0:T(8,128)} async-done(((f32[192,64,128]{2,1,0:T(8,128)}), f32[4,64,128]{2,1,0:T(8,128)}) %reduce-scatter.2.cloned.1.call-update) | async-done | bytes 131088 | tf_op jit(solution)/shard_map/reduce_scatter | solution.py:20
  460.1 1.5 convert_element_type.10
  461.6 0.0 all-gather.2.cloned.1.call-update
  461.7 48.7 %all-gather.2.cloned.1.call-done = bf16[4,64,2048]{2,1,0:T(8,128)(2,1)} async-done(((bf16[4,64,128]{2,1,0:T(8,128)(2,1)}), bf16[4,64,2048]{2,1,0:T(8,128)(2,1)}) %all-gather.2.cloned.1.call-update) | async-done | bytes 1048592 | tf_op jit(solution)/shard_map/all_gather | solution.py:24
  510.4 0.0 copy-done
  510.4 2.3 convolution_convert_fusion
Async XLA Ops:
  6.5 503.8 %copy-start = (bf16[128,2048]{1,0:T(8,128)(2,1)S(1)}, bf16[128,2048]{1,0:T(8,128)(2,1)}, u32[]{:S(2)}) copy-start(bf16[128,2048]{1,0:T(8,128)(2,1)} %param.7) | copy-start | bytes 1572868
  6.5 453.6 %reduce-scatter.2.cloned.1.call-start = ((), (), s32[]{:S(2)}) async-start(), calls=%async_computation.1 | async-start | bytes 6422528 | tf_op jit(solution)/shard_map/reduce_scatter | solution.py:20
  17.6 492.8 %all-gather.2.cloned.1.call-start = ((), (), s32[]{:S(2)}) async-start(), calls=%async_computation.2 | async-start | bytes 1114112 | tf_op jit(solution)/shard_map/all_gather | solution.py:24
Sparse Core Ops, SparseCore 0:
  17.7 442.3 reduce-scatter.1
  462.4 47.8 all-gather.1
where the time goes:
time: 520 us; the launch traced here: 519 us
  waiting for transfers between devices  491 us (94%)
  between operations  13.4 us (3%)
  local copies, waits for them, and re-layouts  6.55 us (1%)
  matrix products  6.01 us (1%)
    reduce_scatter x1, waiting for transfers between devices, shards(): lax.psum_scatter(partial_term, 'col', scatter_dimension=0, tiled=True)  442 us
    all_gather x1, waiting for transfers between devices, shards(): lax.all_gather(occupied_half, 'row', axis=2, tiled=True)  48.7 us
  transfers between devices with their start and end apart: 2, of which 2 were waited for; matrix products, arithmetic and copies ran while one was open for 0% of the time, Pallas kernels for 0%

commit v1 on v0

v1 whole, which is shorter than its diff:
```python
import heapq

import jax
import jax.numpy as jnp
from jax import lax
from jax.experimental import pallas as pl
from jax.experimental.pallas import tpu as pltpu
from jax.sharding import PartitionSpec as P

MESH = pl.DeviceIdType.MESH
NZ, NX, NY = 12, 4, 8
NJ, NP, M, N, S = 4, 64, 128, 256, 192
F32, BF16 = jnp.float32, jnp.bfloat16

PIECES = [
    ("A", 12, "ring"),
    ("B", 12, "two"),
    ("A", 12, "ring"),
    ("B", 8, "two"),
    ("B", 12, "two"),
    ("B", 8, "two"),
]

PER_BYTE, LATENCY, PER_HOP = 2.0 / 91e3, 2.3, 0.45


def halves(n, flip):
    far, near = n // 2, (n - 1) // 2
    return (near, far) if flip else (far, near)


def plan(pieces):
    shapes, copies = {}, 0
    for i, (kind, width, way) in enumerate(pieces):
        rows = NJ * width
        if kind == "A":
            shapes[f"zpart{i}"] = pltpu.VMEM((NZ, NX * rows, M), F32)
            shapes[f"xpart{i}"] = pltpu.VMEM((NX, rows, M), F32)
            shapes[f"xsend{i}"] = pltpu.VMEM((NX, rows, M), BF16)
            shapes[f"xrecv{i}"] = pltpu.VMEM((NX - 1, rows, M), BF16)
            copies += NX - 1
        else:
            shapes[f"xpart{i}"] = pltpu.VMEM((NX, NZ * rows, M), F32)
            shapes[f"zpart{i}"] = pltpu.VMEM((NZ, rows, M), F32)
            for side, hops in enumerate(halves(NX, i % 2)):
                if hops:
                    shapes[f"xs{i}{side}"] = pltpu.VMEM((hops, NZ * rows, M), BF16)
                    shapes[f"xr{i}{side}"] = pltpu.VMEM((hops, NZ * rows, M), BF16)
            copies += NX - 1
        if way == "ring":
            zrows = rows * (NX if kind == "A" else 1)
            for side, hops in enumerate(halves(NZ, i % 2)):
                shapes[f"zs{i}{side}"] = pltpu.VMEM((hops, zrows, M), BF16)
                shapes[f"zr{i}{side}"] = pltpu.VMEM((hops, zrows, M), BF16)
            copies += NZ - 1
        else:
            shapes[f"zs{i}"] = pltpu.VMEM((3, NZ // 3, rows, M), BF16)
            shapes[f"zr{i}"] = pltpu.VMEM((2, NZ // 3, rows, M), BF16)
            shapes[f"zt{i}"] = pltpu.VMEM((NZ // 3, rows, M), BF16)
            shapes[f"zu{i}"] = pltpu.VMEM((3, rows, M), BF16)
            copies += 5
        shapes[f"gath{i}"] = pltpu.VMEM((2, NY, rows, M), BF16)
        copies += NY
    shapes["tc"] = pltpu.VMEM((NP, M, N), BF16)
    shapes["go"] = pltpu.VMEM((N, S), BF16)
    shapes["gv"] = pltpu.VMEM((M, 2 * NY * M), BF16)
    shapes["screen"] = pltpu.VMEM((M, N), BF16)
    shapes["gt"] = pltpu.VMEM((2, S, N), BF16)
    shapes["acc"] = pltpu.VMEM((NP * NJ, M), F32)
    shapes["load"] = pltpu.SemaphoreType.DMA((len(pieces) + 2,))
    shapes["sent"] = pltpu.SemaphoreType.DMA((copies,))
    shapes["came"] = pltpu.SemaphoreType.DMA((copies,))
    return shapes


def block_rows(rows):
    for size in (96, 80, 64, 48, 32, 16):
        if rows % size == 0:
            return size


def over_rows(rows, body):
    size = block_rows(rows)
    if rows == size:
        body(pl.ds(0, size))
    else:

        @pl.loop(0, rows // size)
        def _(b):
            body(pl.ds(pl.multiple_of(b * size, size), size))


class Builder:
    def __init__(self, pieces, refs):
        self.pieces, self.refs = pieces, refs
        self.now, self.free, self.handles, self.order, self.heap = 0.0, {}, [], 0, []
        row, col = lax.axis_index("row"), lax.axis_index("col")
        self.y, self.k = row // 2, lax.rem(row, 2)
        self.z, self.x = col // NX, lax.rem(col, NX)

    def at(self, axis, step):
        z, x, y, k = self.z, self.x, self.y, self.k
        if axis == "z":
            z = lax.rem(z + (step + NZ), NZ)
        elif axis == "x":
            x = lax.rem(x + (step + NX), NX)
        elif axis == "y":
            y = lax.rem(y + (step + NY), NY)
        else:
            k = 1 - k
        return (y * 2 + k, z * NX + x)

    def send(self, src, dst, axis, step):
        n = len(self.handles)
        copy = pltpu.make_async_remote_copy(
            src_ref=src,
            dst_ref=dst,
            send_sem=self.refs["sent"].at[n],
            recv_sem=self.refs["came"].at[n],
            device_id=self.at(axis, step),
            device_id_type=MESH,
        )
        copy.start()
        self.handles.append(copy)
        size = 2.0
        for length in src.shape:
            size *= length
        if axis == "k":
            return copy, self.now + 0.8 + size / 400e3
        ring = {"z": NZ, "x": NX, "y": NY}[axis]
        ahead = step % ring
        hops = min(ahead, ring - ahead)
        link = axis + ("+" if ahead * 2 <= ring else "-")
        begin = max(self.now, self.free.get(link, 0.0))
        self.free[link] = begin + hops * size * PER_BYTE
        self.now += 0.05
        return copy, begin + size * PER_BYTE * max(1, hops / 2) + LATENCY + PER_HOP * (hops - 1)

    def work(self, rows):
        self.now += 0.1 + rows / 8 * 0.004

    def push(self, ready, task):
        self.order += 1
        heapq.heappush(self.heap, (ready, self.order, task))

    def run(self):
        while self.heap:
            ready, _, task = heapq.heappop(self.heap)
            self.now = max(self.now, ready)
            for later in task:
                self.push(later, task)
                break

    def chain(self, part, send, recv, axis, ring, hops, sign, arrived):
        me = {"z": self.z, "x": self.x}[axis]
        rows = part.shape[1]
        for t in range(hops):
            owner = lax.rem(me + (sign * (hops - t) + ring), ring)
            if t:
                yield when
                copy.wait_recv()

            def body(block, t=t, owner=owner):
                value = part[owner, block]
                if t:
                    value = value + recv[t - 1, block].astype(F32)
                send[t, block] = value.astype(BF16)

            over_rows(rows, body)
            self.work(rows)
            copy, when = self.send(send.at[t], recv.at[t], axis, sign)
        arrived.append((copy, when, recv.at[hops - 1]))

    def both(self, i, part, name, axis, ring, then):
        arrived = []
        sides = [(side, hops) for side, hops in enumerate(halves(ring, i % 2)) if hops]

        def follow(task):
            yield from task
            if len(arrived) == len(sides):
                self.push(max(a[1] for a in arrived), then(arrived))

        for side, hops in sides:
            send, recv = self.refs[f"{name[0]}s{i}{side}"], self.refs[f"{name[0]}r{i}{side}"]
            task = self.chain(part, send, recv, axis, ring, hops, 1 - 2 * side, arrived)
            self.push(self.now, follow(task))

    def piece(self, i, first):
        kind, width, way = self.pieces[i]
        refs = self.refs
        rows = NJ * width
        refs_tc, screen = refs["tc"], refs["screen"]
        self.loads[i].wait()
        gt = refs["gt"].at[0 if kind == "A" else 1]
        into = refs[f"zpart{i}"] if kind == "A" else refs[f"xpart{i}"]
        blocks = NZ if kind == "A" else NX
        depth = S // blocks

        @pl.loop(0, width // 2)
        def _(q):
            tensor = (refs_tc[pl.ds(first + 2 * q, 2)] * screen[...][None]).reshape(2 * M, N)
            term = lax.dot_general(gt[...], tensor, (((1,), (1,)), ((), ())), preferred_element_type=F32)
            for u in range(2):
                at = pl.ds(pl.multiple_of((2 * q + u) * depth, depth), depth)
                into[:, at, :] = term[:, u * M : (u + 1) * M].reshape(blocks, depth, M)

        self.now += 0.05 * width
        if i == 0:
            pl.semaphore_wait(pltpu.get_barrier_semaphore(), self.peers)
        if kind == "A":
            self.both(i, into, "z", "z", NZ, lambda arrived: self.a_middle(i, first, arrived))
        else:
            self.both(i, into, "x", "x", NX, lambda arrived: self.b_middle(i, first, arrived))
        return
        yield

    def packed(self, value0, value1):
        upper = lax.broadcasted_iota(jnp.int32, value0.shape, 1) < NJ
        low = jnp.where(upper, value0, pltpu.roll(value1, NJ, 1))
        high = jnp.where(upper, pltpu.roll(value0, NJ, 1), value1)
        return low, high

    def repack(self, width, depth, part, owner, arrived, into, also=None):
        groups = depth // 8
        received = [a[2] for a in arrived]

        @pl.loop(0, width // 2)
        def _(q):
            at = pl.ds(pl.multiple_of(q * 2 * depth, 2 * depth), 2 * depth)
            value = part[owner, at]
            for ref in received:
                value = value + ref[at].astype(F32)
            value = value.reshape(2, groups, 8, M)
            low, high = self.packed(value[0], value[1])
            to = pl.ds(pl.multiple_of(q * 8, 8), 8)
            for g in range(groups):
                into[2 * g, to] = low[g]
                into[2 * g + 1, to] = high[g]

    def a_middle(self, i, first, arrived):
        kind, width, way = self.pieces[i]
        rows = NJ * width
        refs = self.refs
        for copy, _, _ in arrived:
            copy.wait_recv()
        xpart, xsend, xrecv = refs[f"xpart{i}"], refs[f"xsend{i}"], refs[f"xrecv{i}"]
        self.repack(width, NX * NJ, refs[f"zpart{i}"], self.z, arrived, xpart)
        xsend[...] = xpart[...].astype(BF16)
        self.work(8 * rows)
        copies = []
        for d in (2, 1, 3):
            to = lax.rem(self.x + d, NX)
            copies.append(self.send(xsend.at[to], xrecv.at[d - 1], "x", d))
        yield max(c[1] for c in copies)
        for copy, _ in copies:
            copy.wait_recv()
        value = xpart[self.x]
        for d in range(NX - 1):
            value = value + xrecv[d].astype(F32)
        yield from self.last(i, first, value)

    def b_middle(self, i, first, arrived):
        kind, width, way = self.pieces[i]
        rows = NJ * width
        refs = self.refs
        for copy, _, _ in arrived:
            copy.wait_recv()
        zpart = refs[f"zpart{i}"]
        self.repack(width, NZ * NJ, refs[f"xpart{i}"], self.x, arrived, zpart)
        self.work(24 * rows)
        if way == "ring":
            self.both(i, zpart, "z", "z", NZ, lambda came: self.b_end(i, first, came))
            return
        zs, zr, zt, zu = (refs[f"{name}{i}"] for name in ("zs", "zr", "zt", "zu"))
        for r in range(3):
            for c in range(NZ // 3):
                zs[r, c] = zpart[3 * c + r].astype(BF16)
        self.work(12 * rows)
        copies = []
        for side, step in enumerate((1, -1)):
            r = lax.rem(self.z + step + NZ, 3)
            copies.append(self.send(zs.at[r], zr.at[side], "z", step))
        yield max(c[1] for c in copies)
        for copy, _ in copies:
            copy.wait_recv()
        mine, home = lax.rem(self.z, 3), self.z // 3
        for c in range(NZ // 3):
            value = zpart[3 * c + mine] + zr[0, c].astype(F32) + zr[1, c].astype(F32)
            zpart[3 * c + mine] = value
            zt[c] = value.astype(BF16)
        self.work(8 * rows)
        copies = []
        for d in (2, 1, 3):
            to = lax.rem(home + d, NZ // 3)
            copies.append(self.send(zt.at[to], zu.at[d - 1], "z", 3 * d))
        yield max(c[1] for c in copies)
        for copy, _ in copies:
            copy.wait_recv()
        value = zpart[self.z]
        for d in range(3):
            value = value + zu[d].astype(F32)
        yield from self.last(i, first, value)

    def b_end(self, i, first, arrived):
        for copy, _, _ in arrived:
            copy.wait_recv()
        value = self.refs[f"zpart{i}"][self.z]
        for _, _, ref in arrived:
            value = value + ref[...].astype(F32)
        yield from self.last(i, first, value)

    def last(self, i, first, value):
        kind, width, way = self.pieces[i]
        rows = NJ * width
        gath = self.refs[f"gath{i}"]
        gath[self.k, self.y] = value.astype(BF16)
        self.work(3 * rows)
        own = gath.at[self.k, self.y]
        copies = [self.send(own, own, "y", d) for d in (4, 3, 5, 2, 6, 1, 7)]
        yield max(c[1] for c in copies)
        for copy, _ in copies:
            copy.wait_recv()
        half = gath.at[self.k]
        copy, when = self.send(half, half, "k", 1)
        yield when
        copy.wait_recv()
        gv = self.refs["gv"]
        total = jnp.zeros((rows, M), F32)
        for y in range(NY):
            left = jnp.concatenate([gath[0, y], gath[1, y]], axis=1)
            right = gv[:, 2 * M * y : 2 * M * (y + 1)]
            total += lax.dot_general(left, right, (((1,), (1,)), ((), ())), preferred_element_type=F32)
        self.refs["acc"][pl.ds(NJ * first, rows)] = total
        self.now += 0.4


def kernel(pieces, names, tensor, mask, occ, virt, out, *scratch):
    refs = dict(zip(names, scratch))
    b = Builder(pieces, refs)
    barrier = pltpu.get_barrier_semaphore()
    reached = [("z", d) for d in (1, -1)] + [("x", d) for d in (1, 2, 3)]
    if any(kind == "B" and way == "two" for kind, _, way in pieces):
        reached += [("z", d) for d in (3, 6, 9)]
    reached += [("y", d) for d in range(1, NY)] + [("k", 1)]
    for axis, step in reached:
        pl.semaphore_signal(barrier, inc=1, device_id=b.at(axis, step), device_id_type=MESH)
    b.peers = len(reached)
    load = refs["load"]
    occ_load = pltpu.make_async_copy(occ, refs["go"], load.at[len(pieces)])
    occ_load.start()
    b.loads, firsts, first = [], [], 0
    for i, (_, width, _) in enumerate(pieces):
        at = pl.ds(first, width)
        b.loads.append(pltpu.make_async_copy(tensor.at[at], refs["tc"].at[at], load.at[i]))
        b.loads[-1].start()
        firsts.append(first)
        first += width
    virt_load = pltpu.make_async_copy(virt, refs["gv"], load.at[len(pieces) + 1])
    virt_load.start()

    down = lax.broadcasted_iota(jnp.int32, (M, N), 0)
    along = lax.broadcasted_iota(jnp.int32, (M, N), 1)
    screen = jnp.zeros((M, N), F32)
    for mb in range(M // 64):
        for nb in range(N // 64):
            inside = (down // 64 == mb) & (along // 64 == nb)
            screen = jnp.where(inside, mask[0, mb, nb].astype(F32), screen)
    refs["screen"][...] = screen.astype(BF16)

    occ_load.wait()
    q = lax.broadcasted_iota(jnp.int32, (S, S), 0)
    s = lax.broadcasted_iota(jnp.int32, (S, S), 1)
    strip = NZ * NJ
    x = sum((q >= strip * c).astype(jnp.int32) for c in range(1, NX))
    rest = q - strip * x
    there = (rest >> 2) * (NX * NJ) + x * NJ + (rest & 3)
    for which, column in enumerate((q, there)):
        pick = (s == column).astype(F32).astype(BF16)
        turned = lax.dot_general(pick, refs["go"][...], (((1,), (1,)), ((), ())), preferred_element_type=F32)
        refs["gt"][which] = turned.astype(BF16)

    for i in range(len(pieces)):
        b.push(0.0, b.piece(i, firsts[i]))
    virt_load.wait()
    b.run()
    for copy in b.handles:
        copy.wait_send()
    for j in range(NJ):
        out[j] = refs["acc"][pl.ds(j, NP, stride=NJ), :].astype(BF16)


def shards(three_centre, block_mask, g_occ, g_virt):
    shapes = plan(PIECES)
    names = tuple(shapes)

    def body(*refs):
        kernel(PIECES, names, *refs)

    return pl.pallas_call(
        body,
        out_shape=jax.ShapeDtypeStruct((NJ, NP, M), BF16),
        in_specs=[
            pl.BlockSpec(memory_space=pl.ANY),
            pl.BlockSpec(memory_space=pltpu.SMEM),
            pl.BlockSpec(memory_space=pl.ANY),
            pl.BlockSpec(memory_space=pl.ANY),
        ],
        out_specs=pl.BlockSpec(memory_space=pltpu.VMEM),
        scratch_shapes=list(shapes.values()),
        compiler_params=pltpu.CompilerParams(
            collective_id=0, has_side_effects=True, vmem_limit_bytes=48 * 1024 * 1024
        ),
    )(three_centre, block_mask, g_occ, g_virt)


def solution(mesh):
    placed = (P(None, "row", "col"), P(None, "row", "col"), P("col", None), P("row", None))
    return jax.shard_map(
        shards, mesh=mesh, in_specs=placed, out_specs=P("col", None, "row"), check_vma=False
    )
```

time: 520 us -> 74.5 us (0.14)
  waiting for transfers between devices: 491 us -> 0 us
  Pallas kernels: 0 us -> 68.7 us
  between operations: 13.4 us -> 0.03 us
  matrix products: 6.01 us -> 0 us
    reduce_scatter x1 -> x0, waiting for transfers between devices: 442 us -> none  [shards(): lax.psum_scatter(partial_term, 'col', scatter_dimension=0, tiled=True)]
    pallas_call x0 -> x1, Pallas kernels: none -> 68.7 us  [shards(): pl.pallas_call(body, out_shape=jax.ShapeDtypeStruct((NJ, NP, M), BF16), i...]
    all_gather x1 -> x0, waiting for transfers between devices: 48.7 us -> none  [shards(): lax.all_gather(occupied_half, 'row', axis=2, tiled=True)]
    dot_general x1 -> x0, local copies, waits for them, and re-layouts: 6.29 us -> none  [shards(): jnp.einsum('pmn,ns->spm', screened, g_occ, preferred_element_type=jnp.flo...]
    dot_general x2 -> x0, matrix products: 6.01 us -> none  [the longest x1 3.72 us: shards(): jnp.einsum('pmn,ns->spm', screened, g_occ, preferred_element_type=jnp.flo...]
    unnamed x2 -> x8, local copies, waits for them, and re-layouts: 0.01 us -> 5.52 us
  transfers between devices with their start and end apart: 2 -> 0, of which waited for: 2 -> 0; matrix products, arithmetic and copies ran while one was open for 0% -> 0% of each run, Pallas kernels for 0% -> 0%
where the time goes in v1:
time: 74.5 us; the launch traced here: 74.3 us
  Pallas kernels  68.7 us (92%)
  local copies, waits for them, and re-layouts  5.52 us (7%)
    pallas_call x1, Pallas kernels, shards(): pl.pallas_call(body, out_shape=jax.ShapeDtypeStruct((NJ, NP, M), BF16), i...  68.7 us
    unnamed x8, local copies, waits for them, and re-layouts  5.52 us

profile of v1, /device:TPU:1, one launch (start us, length us, event | category | flops | bytes accessed | tf_op | source)
XLA Modules:
  0.0 74.3 jit_solution(5028336874022608666)
XLA Ops:
  0.0 1.0 %copy.5.refs_2_ = bf16[256,192]{1,0:T(8,128)(2,1)S(1)} copy(bf16[256,192]{0,1:T(8,128)(2,1)} %param.6) | data formatting | bytes 196608 | tf_op args[2]
  1.0 0.0 copy-start
  1.0 2.2 %copy-done = bf16[64,128,256]{2,1,0:T(8,128)(2,1)S(1)} copy-done((bf16[64,128,256]{2,1,0:T(8,128)(2,1)S(1)}, bf16[64,128,256]{2,1,0:T(8,128)(2,1)}, u32[]{:S(2)}) %copy-start) | copy-done | bytes 4194328
  3.2 0.0 copy-start.1
  3.2 1.0 %copy-done.1 = bf16[128,2048]{1,0:T(8,128)(2,1)S(1)} copy-done((bf16[128,2048]{1,0:T(8,128)(2,1)S(1)}, bf16[128,2048]{1,0:T(8,128)(2,1)}, u32[]{:S(2)}) %copy-start.1) | copy-done | bytes 524312
  4.2 0.0 copy-start.2
  4.2 0.7 copy-done.2
  4.9 68.7 %shard_map.46 = bf16[4,64,128]{2,1,0:T(8,128)(2,1)S(1)} custom-call(bf16[64,128,256]{2,1,0:T(8,128)(2,1)S(1)} %copy-done, s32[1,2,4]{2,1,0:T(2,128)S(1)} %copy-done.2, bf16[256,192]{1,0:T(8,128)(2,1)S(1)} %copy.5.refs_2_, bf16[128,2048]{1,0:T(8,128)(2,1)S(1)} %copy-done.1), custom_call_target="tpu_custom_call" | custom-call | tf_op jit(solution)/shard_map/pallas_call | solution.py:399
  73.6 0.6 copy.7
Async XLA Ops:
  1.0 2.2 %copy-start = (bf16[64,128,256]{2,1,0:T(8,128)(2,1)S(1)}, bf16[64,128,256]{2,1,0:T(8,128)(2,1)}, u32[]{:S(2)}) copy-start(bf16[64,128,256]{2,1,0:T(8,128)(2,1)} %refs_0_.1) | copy-start | bytes 12582916
  3.2 1.0 %copy-start.1 = (bf16[128,2048]{1,0:T(8,128)(2,1)S(1)}, bf16[128,2048]{1,0:T(8,128)(2,1)}, u32[]{:S(2)}) copy-start(bf16[128,2048]{1,0:T(8,128)(2,1)} %refs_3_.1) | copy-start | bytes 1572868
  4.2 0.7 copy-start.2

commit v2 on v1

--- a/solution.py
+++ b/solution.py
@@ -7,21 +7,22 @@
 from jax.experimental.pallas import tpu as pltpu
 from jax.sharding import PartitionSpec as P
 
+UNROLL = (4, 3, 2, 1)
 MESH = pl.DeviceIdType.MESH
 NZ, NX, NY = 12, 4, 8
 NJ, NP, M, N, S = 4, 64, 128, 256, 192
 F32, BF16 = jnp.float32, jnp.bfloat16
 
 PIECES = [
-    ("A", 12, "ring"),
-    ("B", 12, "two"),
-    ("A", 12, "ring"),
-    ("B", 8, "two"),
-    ("B", 12, "two"),
-    ("B", 8, "two"),
+    ("A", 16, "ring", "direct", "half", 0, 0, 4.3),
+    ("B", 12, "two", "direct", "half", 1, 0, 5.8),
+    ("B", 12, "two", "ring", "direct", 1, 1, 9.7),
+    ("B", 8, "two", "ring", "direct", 0, 1, 13.8),
+    ("A", 16, "ring", "direct", "half", 0, 0, 0.0),
 ]
 
-PER_BYTE, LATENCY, PER_HOP = 2.0 / 91e3, 2.3, 0.45
+PER_BYTE, LATENCY, PER_HOP = 2.0 / 97e3, 1.76, 0.45
+PER_RI, PER_SEND, PER_STEP, PER_TILE = 0.077, 0.13, 0.11, 0.005
 
 
 def halves(n, flip):
@@ -31,7 +32,7 @@
 
 def plan(pieces):
     shapes, copies = {}, 0
-    for i, (kind, width, way) in enumerate(pieces):
+    for i, (kind, width, way, xway, yway, zflip, xflip, _) in enumerate(pieces):
         rows = NJ * width
         if kind == "A":
             shapes[f"zpart{i}"] = pltpu.VMEM((NZ, NX * rows, M), F32)
@@ -42,14 +43,17 @@
         else:
             shapes[f"xpart{i}"] = pltpu.VMEM((NX, NZ * rows, M), F32)
             shapes[f"zpart{i}"] = pltpu.VMEM((NZ, rows, M), F32)
-            for side, hops in enumerate(halves(NX, i % 2)):
-                if hops:
+            if xway == "ring":
+                for side, hops in enumerate(halves(NX, xflip)):
                     shapes[f"xs{i}{side}"] = pltpu.VMEM((hops, NZ * rows, M), BF16)
                     shapes[f"xr{i}{side}"] = pltpu.VMEM((hops, NZ * rows, M), BF16)
+            else:
+                shapes[f"xsend{i}"] = pltpu.VMEM((NX, NZ * rows, M), BF16)
+                shapes[f"xrecv{i}"] = pltpu.VMEM((NX - 1, NZ * rows, M), BF16)
             copies += NX - 1
         if way == "ring":
             zrows = rows * (NX if kind == "A" else 1)
-            for side, hops in enumerate(halves(NZ, i % 2)):
+            for side, hops in enumerate(halves(NZ, zflip)):
                 shapes[f"zs{i}{side}"] = pltpu.VMEM((hops, zrows, M), BF16)
                 shapes[f"zr{i}{side}"] = pltpu.VMEM((hops, zrows, M), BF16)
             copies += NZ - 1
@@ -60,23 +64,27 @@
             shapes[f"zu{i}"] = pltpu.VMEM((3, rows, M), BF16)
             copies += 5
         shapes[f"gath{i}"] = pltpu.VMEM((2, NY, rows, M), BF16)
-        copies += NY
+        copies += NY if yway == "direct" else 6
     shapes["tc"] = pltpu.VMEM((NP, M, N), BF16)
-    shapes["go"] = pltpu.VMEM((N, S), BF16)
+    shapes["flags"] = pltpu.SMEM((1, M // 64, N // 64), jnp.int32)
     shapes["gv"] = pltpu.VMEM((M, 2 * NY * M), BF16)
     shapes["screen"] = pltpu.VMEM((M, N), BF16)
     shapes["gt"] = pltpu.VMEM((2, S, N), BF16)
     shapes["acc"] = pltpu.VMEM((NP * NJ, M), F32)
-    shapes["load"] = pltpu.SemaphoreType.DMA((len(pieces) + 2,))
+    shapes["load"] = pltpu.SemaphoreType.DMA((len(pieces) + 3,))
     shapes["sent"] = pltpu.SemaphoreType.DMA((copies,))
     shapes["came"] = pltpu.SemaphoreType.DMA((copies,))
     return shapes
 
 
 def block_rows(rows):
-    for size in (96, 80, 64, 48, 32, 16):
+    for size in (256, 240, 224, 208, 192, 176, 160, 144, 128, 112, 96, 80, 64, 48, 32, 16):
         if rows % size == 0:
             return size
+
+
+def unrolled(count):
+    return next(size for size in UNROLL if count % size == 0)
 
 
 def over_rows(rows, body):
@@ -93,7 +101,8 @@
 class Builder:
     def __init__(self, pieces, refs):
         self.pieces, self.refs = pieces, refs
-        self.now, self.free, self.handles, self.order, self.heap = 0.0, {}, [], 0, []
+        self.greeted = False
+        self.now, self.free, self.handles, self.order, self.heap = 2.5, {}, [], 0, []
         row, col = lax.axis_index("row"), lax.axis_index("col")
         self.y, self.k = row // 2, lax.rem(row, 2)
         self.z, self.x = col // NX, lax.rem(col, NX)
@@ -125,19 +134,22 @@
         size = 2.0
         for length in src.shape:
             size *= length
+        self.now += PER_SEND
         if axis == "k":
             return copy, self.now + 0.8 + size / 400e3
         ring = {"z": NZ, "x": NX, "y": NY}[axis]
         ahead = step % ring
         hops = min(ahead, ring - ahead)
         link = axis + ("+" if ahead * 2 <= ring else "-")
-        begin = max(self.now, self.free.get(link, 0.0))
-        self.free[link] = begin + hops * size * PER_BYTE
-        self.now += 0.05
+        begin = self.now
+        for one, part in ((axis + "+", 0.5), (axis + "-", 0.5)) if ahead * 2 == ring else ((link, 1.0),):
+            free = max(self.now, self.free.get(one, 0.0))
+            self.free[one] = free + part * hops * size * PER_BYTE
+            begin = max(begin, free)
         return copy, begin + size * PER_BYTE * max(1, hops / 2) + LATENCY + PER_HOP * (hops - 1)
 
     def work(self, rows):
-        self.now += 0.1 + rows / 8 * 0.004
+        self.now += PER_STEP + rows / 8 * PER_TILE
 
     def push(self, ready, task):
         self.order += 1
@@ -171,9 +183,9 @@
             copy, when = self.send(send.at[t], recv.at[t], axis, sign)
         arrived.append((copy, when, recv.at[hops - 1]))
 
-    def both(self, i, part, name, axis, ring, then):
+    def both(self, i, part, axis, ring, flip, then):
         arrived = []
-        sides = [(side, hops) for side, hops in enumerate(halves(ring, i % 2)) if hops]
+        sides = list(enumerate(halves(ring, flip)))
 
         def follow(task):
             yield from task
@@ -181,12 +193,12 @@
                 self.push(max(a[1] for a in arrived), then(arrived))
 
         for side, hops in sides:
-            send, recv = self.refs[f"{name[0]}s{i}{side}"], self.refs[f"{name[0]}r{i}{side}"]
+            send, recv = self.refs[f"{axis}s{i}{side}"], self.refs[f"{axis}r{i}{side}"]
             task = self.chain(part, send, recv, axis, ring, hops, 1 - 2 * side, arrived)
             self.push(self.now, follow(task))
 
     def piece(self, i, first):
-        kind, width, way = self.pieces[i]
+        kind, width, way, xway, yway, zflip, xflip, _ = self.pieces[i]
         refs = self.refs
         rows = NJ * width
         refs_tc, screen = refs["tc"], refs["screen"]
@@ -196,7 +208,7 @@
         blocks = NZ if kind == "A" else NX
         depth = S // blocks
 
-        @pl.loop(0, width // 2)
+        @pl.loop(0, width // 2, unroll=unrolled(width // 2))
         def _(q):
             tensor = (refs_tc[pl.ds(first + 2 * q, 2)] * screen[...][None]).reshape(2 * M, N)
             term = lax.dot_general(gt[...], tensor, (((1,), (1,)), ((), ())), preferred_element_type=F32)
@@ -204,13 +216,28 @@
                 at = pl.ds(pl.multiple_of((2 * q + u) * depth, depth), depth)
                 into[:, at, :] = term[:, u * M : (u + 1) * M].reshape(blocks, depth, M)
 
-        self.now += 0.05 * width
-        if i == 0:
+        self.now += PER_RI * width
+        if not self.handles and not self.greeted:
+            self.greeted = True
             pl.semaphore_wait(pltpu.get_barrier_semaphore(), self.peers)
         if kind == "A":
-            self.both(i, into, "z", "z", NZ, lambda arrived: self.a_middle(i, first, arrived))
+            self.both(i, into, "z", NZ, zflip, lambda arrived: self.a_middle(i, first, arrived))
+        elif xway == "ring":
+            self.both(i, into, "x", NX, xflip, lambda arrived: self.b_middle(i, first, arrived))
         else:
-            self.both(i, into, "x", "x", NX, lambda arrived: self.b_middle(i, first, arrived))
+            send, recv = refs[f"xsend{i}"], refs[f"xrecv{i}"]
+            arrived = []
+            for d in (2, 1, 3):
+                to = lax.rem(self.x + d, NX)
+
+                def body(block, to=to):
+                    send[to, block] = into[to, block].astype(BF16)
+
+                over_rows(NZ * NJ * width, body)
+                self.work(NZ * NJ * width)
+                copy, when = self.send(send.at[to], recv.at[d - 1], "x", d)
+                arrived.append((copy, when, recv.at[d - 1]))
+            self.push(max(a[1] for a in arrived), self.b_middle(i, first, arrived))
         return
         yield
 
@@ -224,7 +251,7 @@
         groups = depth // 8
         received = [a[2] for a in arrived]
 
-        @pl.loop(0, width // 2)
+        @pl.loop(0, width // 2, unroll=unrolled(width // 2))
         def _(q):
             at = pl.ds(pl.multiple_of(q * 2 * depth, 2 * depth), 2 * depth)
             value = part[owner, at]
@@ -238,7 +265,7 @@
                 into[2 * g + 1, to] = high[g]
 
     def a_middle(self, i, first, arrived):
-        kind, width, way = self.pieces[i]
+        kind, width, way, xway, yway, zflip, xflip, _ = self.pieces[i]
         rows = NJ * width
         refs = self.refs
         for copy, _, _ in arrived:
@@ -260,7 +287,7 @@
         yield from self.last(i, first, value)
 
     def b_middle(self, i, first, arrived):
-        kind, width, way = self.pieces[i]
+        kind, width, way, xway, yway, zflip, xflip, _ = self.pieces[i]
         rows = NJ * width
         refs = self.refs
         for copy, _, _ in arrived:
@@ -269,7 +296,7 @@
         self.repack(width, NZ * NJ, refs[f"xpart{i}"], self.x, arrived, zpart)
         self.work(24 * rows)
         if way == "ring":
-            self.both(i, zpart, "z", "z", NZ, lambda came: self.b_end(i, first, came))
+            self.both(i, zpart, "z", NZ, zflip, lambda came: self.b_end(i, first, came))
             return
         zs, zr, zt, zu = (refs[f"{name}{i}"] for name in ("zs", "zr", "zt", "zu"))
         for r in range(3):
@@ -310,24 +337,35 @@
         yield from self.last(i, first, value)
 
     def last(self, i, first, value):
-        kind, width, way = self.pieces[i]
+        kind, width, way, xway, yway, zflip, xflip, _ = self.pieces[i]
         rows = NJ * width
         gath = self.refs[f"gath{i}"]
-        gath[self.k, self.y] = value.astype(BF16)
+        home = lax.rem(self.y, 2) * 4 + lax.rem(self.y // 2, 2) * 2 + self.y // 4
+        gath[self.k, home] = value.astype(BF16)
         self.work(3 * rows)
-        own = gath.at[self.k, self.y]
-        copies = [self.send(own, own, "y", d) for d in (4, 3, 5, 2, 6, 1, 7)]
+        own = gath.at[self.k, home]
+        steps = (4, 2, 6) if yway == "half" else (4, 3, 5, 2, 6, 1, 7)
+        copies = [self.send(own, own, "y", d) for d in steps]
         yield max(c[1] for c in copies)
         for copy, _ in copies:
             copy.wait_recv()
+        if yway == "half":
+            copies = []
+            for side, step in enumerate((1, -1)):
+                both = gath.at[self.k, pl.ds(lax.rem(self.y, 2) * 4 + 2 * side, 2)]
+                copies.append(self.send(both, both, "y", step))
+            yield max(c[1] for c in copies)
+            for copy, _ in copies:
+                copy.wait_recv()
         half = gath.at[self.k]
         copy, when = self.send(half, half, "k", 1)
         yield when
         copy.wait_recv()
         gv = self.refs["gv"]
         total = jnp.zeros((rows, M), F32)
-        for y in range(NY):
-            left = jnp.concatenate([gath[0, y], gath[1, y]], axis=1)
+        for slot in range(NY):
+            y = slot // 4 + 2 * (slot // 2 % 2) + 4 * (slot % 2)
+            left = jnp.concatenate([gath[0, slot], gath[1, slot]], axis=1)
             right = gv[:, 2 * M * y : 2 * M * (y + 1)]
             total += lax.dot_general(left, right, (((1,), (1,)), ((), ())), preferred_element_type=F32)
         self.refs["acc"][pl.ds(NJ * first, rows)] = total
@@ -339,32 +377,36 @@
     b = Builder(pieces, refs)
     barrier = pltpu.get_barrier_semaphore()
     reached = [("z", d) for d in (1, -1)] + [("x", d) for d in (1, 2, 3)]
-    if any(kind == "B" and way == "two" for kind, _, way in pieces):
+    if any(kind == "B" and way == "two" for kind, _, way, *_ in pieces):
         reached += [("z", d) for d in (3, 6, 9)]
     reached += [("y", d) for d in range(1, NY)] + [("k", 1)]
     for axis, step in reached:
         pl.semaphore_signal(barrier, inc=1, device_id=b.at(axis, step), device_id_type=MESH)
     b.peers = len(reached)
     load = refs["load"]
-    occ_load = pltpu.make_async_copy(occ, refs["go"], load.at[len(pieces)])
+    occ_load = pltpu.make_async_copy(occ, refs["gt"].at[0], load.at[len(pieces)])
     occ_load.start()
+    mask_load = pltpu.make_async_copy(mask, refs["flags"], load.at[len(pieces) + 2])
+    mask_load.start()
     b.loads, firsts, first = [], [], 0
-    for i, (_, width, _) in enumerate(pieces):
+    for i, (_, width, *_) in enumerate(pieces):
         at = pl.ds(first, width)
         b.loads.append(pltpu.make_async_copy(tensor.at[at], refs["tc"].at[at], load.at[i]))
-        b.loads[-1].start()
         firsts.append(first)
         first += width
+    for i in sorted(range(len(pieces)), key=lambda i: pieces[i][7]):
+        b.loads[i].start()
     virt_load = pltpu.make_async_copy(virt, refs["gv"], load.at[len(pieces) + 1])
     virt_load.start()
 
     down = lax.broadcasted_iota(jnp.int32, (M, N), 0)
     along = lax.broadcasted_iota(jnp.int32, (M, N), 1)
     screen = jnp.zeros((M, N), F32)
+    mask_load.wait()
     for mb in range(M // 64):
         for nb in range(N // 64):
             inside = (down // 64 == mb) & (along // 64 == nb)
-            screen = jnp.where(inside, mask[0, mb, nb].astype(F32), screen)
+            screen = jnp.where(inside, refs["flags"][0, mb, nb].astype(F32), screen)
     refs["screen"][...] = screen.astype(BF16)
 
     occ_load.wait()
@@ -374,13 +416,12 @@
     x = sum((q >= strip * c).astype(jnp.int32) for c in range(1, NX))
     rest = q - strip * x
     there = (rest >> 2) * (NX * NJ) + x * NJ + (rest & 3)
-    for which, column in enumerate((q, there)):
-        pick = (s == column).astype(F32).astype(BF16)
-        turned = lax.dot_general(pick, refs["go"][...], (((1,), (1,)), ((), ())), preferred_element_type=F32)
-        refs["gt"][which] = turned.astype(BF16)
+    pick = (s == there).astype(F32).astype(BF16)
+    turned = lax.dot_general(pick, refs["gt"][0], (((1,), (0,)), ((), ())), preferred_element_type=F32)
+    refs["gt"][1] = turned.astype(BF16)
 
     for i in range(len(pieces)):
-        b.push(0.0, b.piece(i, firsts[i]))
+        b.push(pieces[i][7], b.piece(i, firsts[i]))
     virt_load.wait()
     b.run()
     for copy in b.handles:
@@ -400,17 +441,17 @@
         body,
         out_shape=jax.ShapeDtypeStruct((NJ, NP, M), BF16),
         in_specs=[
-            pl.BlockSpec(memory_space=pl.ANY),
-            pl.BlockSpec(memory_space=pltpu.SMEM),
-            pl.BlockSpec(memory_space=pl.ANY),
-            pl.BlockSpec(memory_space=pl.ANY),
+            pl.BlockSpec(memory_space=pltpu.HBM),
+            pl.BlockSpec(memory_space=pltpu.HBM),
+            pl.BlockSpec(memory_space=pltpu.HBM),
+            pl.BlockSpec(memory_space=pltpu.HBM),
         ],
         out_specs=pl.BlockSpec(memory_space=pltpu.VMEM),
         scratch_shapes=list(shapes.values()),
         compiler_params=pltpu.CompilerParams(
             collective_id=0, has_side_effects=True, vmem_limit_bytes=48 * 1024 * 1024
         ),
-    )(three_centre, block_mask, g_occ, g_virt)
+    )(three_centre, block_mask, g_occ.T, g_virt)
 
 
 def solution(mesh):

time: 74.5 us -> 69.5 us (0.933)
  Pallas kernels: 68.7 us -> 63.8 us
    pallas_call x1, Pallas kernels: 68.7 us -> 63.8 us  [shards(): pl.pallas_call(body, out_shape=jax.ShapeDtypeStruct((NJ, NP, M), BF16), i...]
    unnamed x8 -> x9, local copies, waits for them, and re-layouts: 5.52 us -> 5.43 us
where the time goes in v2:
time: 69.5 us; the launch traced here: 69.2 us
  Pallas kernels  63.8 us (92%)
  local copies, waits for them, and re-layouts  5.43 us (8%)
    pallas_call x1, Pallas kernels, shards(): pl.pallas_call(body, out_shape=jax.ShapeDtypeStruct((NJ, NP, M), BF16), i...  63.8 us
    unnamed x9, local copies, waits for them, and re-layouts  5.43 us

profile of v2, /device:TPU:1, one launch (start us, length us, event | category | flops | bytes accessed | tf_op | source)
XLA Modules:
  0.0 69.2 jit_solution(8529910326269885338)
XLA Ops:
  0.0 0.0 copy-start
  0.0 2.2 %copy-done = bf16[64,128,256]{2,1,0:T(8,128)(2,1)S(1)} copy-done((bf16[64,128,256]{2,1,0:T(8,128)(2,1)S(1)}, bf16[64,128,256]{2,1,0:T(8,128)(2,1)}, u32[]{:S(2)}) %copy-start) | copy-done | bytes 4194328
  2.2 0.0 copy-start.1
  2.2 1.0 %copy-done.1 = bf16[128,2048]{1,0:T(8,128)(2,1)S(1)} copy-done((bf16[128,2048]{1,0:T(8,128)(2,1)S(1)}, bf16[128,2048]{1,0:T(8,128)(2,1)}, u32[]{:S(2)}) %copy-start.1) | copy-done | bytes 524312
  3.2 0.0 copy-start.2
  3.2 0.9 %copy-done.2 = bf16[256,192]{0,1:T(8,128)(2,1)S(1)} copy-done((bf16[256,192]{0,1:T(8,128)(2,1)S(1)}, bf16[256,192]{0,1:T(8,128)(2,1)}, u32[]{:S(2)}) %copy-start.2) | copy-done | bytes 98328
  4.1 0.0 copy-start.3
  4.1 0.7 copy-done.3
  4.8 63.8 %shard_map.46 = bf16[4,64,128]{2,1,0:T(8,128)(2,1)S(1)} custom-call(bf16[64,128,256]{2,1,0:T(8,128)(2,1)S(1)} %copy-done, s32[1,2,4]{2,1,0:T(2,128)S(1)} %copy-done.3, bf16[192,256]{1,0:T(8,128)(2,1)S(1)} %bitcast.1, bf16[128,2048]{1,0:T(8,128)(2,1)S(1)} %copy-done.1), custom_call_target="tpu_custom_call" | custom-call | tf_op jit(solution)/shard_map/pallas_call | solution.py:440
  68.6 0.6 copy.6
Async XLA Ops:
  0.0 2.2 %copy-start = (bf16[64,128,256]{2,1,0:T(8,128)(2,1)S(1)}, bf16[64,128,256]{2,1,0:T(8,128)(2,1)}, u32[]{:S(2)}) copy-start(bf16[64,128,256]{2,1,0:T(8,128)(2,1)} %refs_0_.1) | copy-start | bytes 12582916
  2.2 1.0 %copy-start.1 = (bf16[128,2048]{1,0:T(8,128)(2,1)S(1)}, bf16[128,2048]{1,0:T(8,128)(2,1)}, u32[]{:S(2)}) copy-start(bf16[128,2048]{1,0:T(8,128)(2,1)} %refs_3_.1) | copy-start | bytes 1572868
  3.2 0.9 %copy-start.2 = (bf16[256,192]{0,1:T(8,128)(2,1)S(1)}, bf16[256,192]{0,1:T(8,128)(2,1)}, u32[]{:S(2)}) copy-start(bf16[256,192]{0,1:T(8,128)(2,1)} %param.6) | copy-start | bytes 294916
  4.1 0.7 copy-start.3

commit v3 on v2

--- a/solution.py
+++ b/solution.py
@@ -8,21 +8,22 @@
 from jax.sharding import PartitionSpec as P
 
 UNROLL = (4, 3, 2, 1)
+RETIRE = 10.0
 MESH = pl.DeviceIdType.MESH
 NZ, NX, NY = 12, 4, 8
 NJ, NP, M, N, S = 4, 64, 128, 256, 192
 F32, BF16 = jnp.float32, jnp.bfloat16
 
 PIECES = [
-    ("A", 16, "ring", "direct", "half", 0, 0, 4.3),
-    ("B", 12, "two", "direct", "half", 1, 0, 5.8),
-    ("B", 12, "two", "ring", "direct", 1, 1, 9.7),
-    ("B", 8, "two", "ring", "direct", 0, 1, 13.8),
-    ("A", 16, "ring", "direct", "half", 0, 0, 0.0),
+    ("A", 12, "ring", "direct", "direct", 0, 0, 0.0),
+    ("A", 12, "ring", "direct", "direct", 1, 0, 1.0),
+    ("B", 12, "two", "ring", "direct", 1, 1, 0.0),
+    ("B", 12, "two", "ring", "direct", 0, 0, 4.0),
+    ("B", 16, "two", "ring", "direct", 0, 0, 8.0),
 ]
 
 PER_BYTE, LATENCY, PER_HOP = 2.0 / 97e3, 1.76, 0.45
-PER_RI, PER_SEND, PER_STEP, PER_TILE = 0.077, 0.13, 0.11, 0.005
+PER_RI, PER_SEND, PER_STEP, PER_TILE = 0.03, 0.13, 0.11, 0.004
 
 
 def halves(n, flip):
@@ -57,6 +58,12 @@
                 shapes[f"zs{i}{side}"] = pltpu.VMEM((hops, zrows, M), BF16)
                 shapes[f"zr{i}{side}"] = pltpu.VMEM((hops, zrows, M), BF16)
             copies += NZ - 1
+        elif way == "skip":
+            zrows = rows * (NX if kind == "A" else 1)
+            for side in range(2):
+                shapes[f"zs{i}{side}"] = pltpu.VMEM((6, zrows, M), BF16)
+                shapes[f"zr{i}{side}"] = pltpu.VMEM((6, zrows, M), BF16)
+            copies += 7
         else:
             shapes[f"zs{i}"] = pltpu.VMEM((3, NZ // 3, rows, M), BF16)
             shapes[f"zr{i}"] = pltpu.VMEM((2, NZ // 3, rows, M), BF16)
@@ -101,7 +108,7 @@
 class Builder:
     def __init__(self, pieces, refs):
         self.pieces, self.refs = pieces, refs
-        self.greeted = False
+        self.greeted, self.retired = False, 0
         self.now, self.free, self.handles, self.order, self.heap = 2.5, {}, [], 0, []
         row, col = lax.axis_index("row"), lax.axis_index("col")
         self.y, self.k = row // 2, lax.rem(row, 2)
@@ -130,7 +137,7 @@
             device_id_type=MESH,
         )
         copy.start()
-        self.handles.append(copy)
+        self.handles.append((copy, self.now))
         size = 2.0
         for length in src.shape:
             size *= length
@@ -158,6 +165,12 @@
     def run(self):
         while self.heap:
             ready, _, task = heapq.heappop(self.heap)
+            while self.now < ready and self.retired < len(self.handles):
+                copy, sent = self.handles[self.retired]
+                if sent + RETIRE > self.now:
+                    break
+                copy.wait_send()
+                self.retired += 1
             self.now = max(self.now, ready)
             for later in task:
                 self.push(later, task)
@@ -197,12 +210,67 @@
             task = self.chain(part, send, recv, axis, ring, hops, 1 - 2 * side, arrived)
             self.push(self.now, follow(task))
 
+    def stride(self, part, send, recv, far, sign, arrived):
+        rows = part.shape[1]
+        for t, ahead in enumerate((5, 3, 1)):
+            owner = lax.rem(self.z + (sign * ahead + NZ), NZ)
+
+            def body(block, t=t, owner=owner):
+                send[t, block] = part[owner, block].astype(BF16)
+
+            over_rows(rows, body)
+        self.work(3 * rows)
+        raw, when = self.send(send.at[pl.ds(0, 3)], recv.at[pl.ds(0, 3)], "z", sign)
+        copy = None
+        for t, ahead in enumerate((6, 4, 2)):
+            if t == 0 and not far:
+                continue
+            if t:
+                yield when
+                if t == 1:
+                    raw.wait_recv()
+                if copy is not None:
+                    copy.wait_recv()
+            owner = lax.rem(self.z + (sign * ahead + NZ), NZ)
+            before = t > 1 or (t == 1 and far)
+
+            def body(block, t=t, owner=owner, before=before):
+                value = part[owner, block]
+                if t:
+                    value = value + recv[t - 1, block].astype(F32)
+                if before:
+                    value = value + recv[t + 2, block].astype(F32)
+                send[t + 3, block] = value.astype(BF16)
+
+            over_rows(rows, body)
+            self.work(1.5 * rows)
+            copy, later = self.send(send.at[t + 3], recv.at[t + 3], "z", 2 * sign)
+            when = later if t else max(when, later)
+        arrived.append((copy, when, recv.at[5]))
+        arrived.append((None, when, recv.at[2]))
+
+    def strides(self, i, part, flip, then):
+        arrived = []
+
+        def follow(task):
+            yield from task
+            if len(arrived) == 4:
+                self.push(max(a[1] for a in arrived), then(arrived))
+
+        for side in range(2):
+            send, recv = self.refs[f"zs{i}{side}"], self.refs[f"zr{i}{side}"]
+            task = self.stride(part, send, recv, side == flip, 1 - 2 * side, arrived)
+            self.push(self.now, follow(task))
+
     def piece(self, i, first):
         kind, width, way, xway, yway, zflip, xflip, _ = self.pieces[i]
         refs = self.refs
         rows = NJ * width
         refs_tc, screen = refs["tc"], refs["screen"]
         self.loads[i].wait()
+        for copy in self.later:
+            copy.start()
+        self.later = []
         gt = refs["gt"].at[0 if kind == "A" else 1]
         into = refs[f"zpart{i}"] if kind == "A" else refs[f"xpart{i}"]
         blocks = NZ if kind == "A" else NX
@@ -220,7 +288,9 @@
         if not self.handles and not self.greeted:
             self.greeted = True
             pl.semaphore_wait(pltpu.get_barrier_semaphore(), self.peers)
-        if kind == "A":
+        if kind == "A" and way == "skip":
+            self.strides(i, into, zflip, lambda arrived: self.a_middle(i, first, arrived))
+        elif kind == "A":
             self.both(i, into, "z", NZ, zflip, lambda arrived: self.a_middle(i, first, arrived))
         elif xway == "ring":
             self.both(i, into, "x", NX, xflip, lambda arrived: self.b_middle(i, first, arrived))
@@ -269,7 +339,8 @@
         rows = NJ * width
         refs = self.refs
         for copy, _, _ in arrived:
-            copy.wait_recv()
+            if copy is not None:
+                copy.wait_recv()
         xpart, xsend, xrecv = refs[f"xpart{i}"], refs[f"xsend{i}"], refs[f"xrecv{i}"]
         self.repack(width, NX * NJ, refs[f"zpart{i}"], self.z, arrived, xpart)
         xsend[...] = xpart[...].astype(BF16)
@@ -297,6 +368,9 @@
         self.work(24 * rows)
         if way == "ring":
             self.both(i, zpart, "z", NZ, zflip, lambda came: self.b_end(i, first, came))
+            return
+        if way == "skip":
+            self.strides(i, zpart, zflip, lambda came: self.b_end(i, first, came))
             return
         zs, zr, zt, zu = (refs[f"{name}{i}"] for name in ("zs", "zr", "zt", "zu"))
         for r in range(3):
@@ -330,7 +404,8 @@
 
     def b_end(self, i, first, arrived):
         for copy, _, _ in arrived:
-            copy.wait_recv()
+            if copy is not None:
+                copy.wait_recv()
         value = self.refs[f"zpart{i}"][self.z]
         for _, _, ref in arrived:
             value = value + ref[...].astype(F32)
@@ -362,6 +437,9 @@
         yield when
         copy.wait_recv()
         gv = self.refs["gv"]
+        if self.virt_load is not None:
+            self.virt_load.wait()
+            self.virt_load = None
         total = jnp.zeros((rows, M), F32)
         for slot in range(NY):
             y = slot // 4 + 2 * (slot // 2 % 2) + 4 * (slot % 2)
@@ -375,14 +453,6 @@
 def kernel(pieces, names, tensor, mask, occ, virt, out, *scratch):
     refs = dict(zip(names, scratch))
     b = Builder(pieces, refs)
-    barrier = pltpu.get_barrier_semaphore()
-    reached = [("z", d) for d in (1, -1)] + [("x", d) for d in (1, 2, 3)]
-    if any(kind == "B" and way == "two" for kind, _, way, *_ in pieces):
-        reached += [("z", d) for d in (3, 6, 9)]
-    reached += [("y", d) for d in range(1, NY)] + [("k", 1)]
-    for axis, step in reached:
-        pl.semaphore_signal(barrier, inc=1, device_id=b.at(axis, step), device_id_type=MESH)
-    b.peers = len(reached)
     load = refs["load"]
     occ_load = pltpu.make_async_copy(occ, refs["gt"].at[0], load.at[len(pieces)])
     occ_load.start()
@@ -394,10 +464,21 @@
         b.loads.append(pltpu.make_async_copy(tensor.at[at], refs["tc"].at[at], load.at[i]))
         firsts.append(first)
         first += width
-    for i in sorted(range(len(pieces)), key=lambda i: pieces[i][7]):
+    order = sorted(range(len(pieces)), key=lambda i: pieces[i][7])
+    for i in order[:2]:
         b.loads[i].start()
-    virt_load = pltpu.make_async_copy(virt, refs["gv"], load.at[len(pieces) + 1])
-    virt_load.start()
+    b.virt_load = pltpu.make_async_copy(virt, refs["gv"], load.at[len(pieces) + 1])
+    b.later = [b.loads[i] for i in order[2:]] + [b.virt_load]
+    barrier = pltpu.get_barrier_semaphore()
+    reached = [("z", d) for d in (1, -1)] + [("x", d) for d in (1, 2, 3)]
+    if any(way == "skip" for _, _, way, *_ in pieces):
+        reached += [("z", d) for d in (2, -2)]
+    if any(kind == "B" and way == "two" for kind, _, way, *_ in pieces):
+        reached += [("z", d) for d in (3, 6, 9)]
+    reached += [("y", d) for d in range(1, NY)] + [("k", 1)]
+    for axis, step in reached:
+        pl.semaphore_signal(barrier, inc=1, device_id=b.at(axis, step), device_id_type=MESH)
+    b.peers = len(reached)
 
     down = lax.broadcasted_iota(jnp.int32, (M, N), 0)
     along = lax.broadcasted_iota(jnp.int32, (M, N), 1)
@@ -422,9 +503,8 @@
 
     for i in range(len(pieces)):
         b.push(pieces[i][7], b.piece(i, firsts[i]))
-    virt_load.wait()
     b.run()
-    for copy in b.handles:
+    for copy, _ in b.handles[b.retired :]:
         copy.wait_send()
     for j in range(NJ):
         out[j] = refs["acc"][pl.ds(j, NP, stride=NJ), :].astype(BF16)
@@ -449,7 +529,7 @@
         out_specs=pl.BlockSpec(memory_space=pltpu.VMEM),
         scratch_shapes=list(shapes.values()),
         compiler_params=pltpu.CompilerParams(
-            collective_id=0, has_side_effects=True, vmem_limit_bytes=48 * 1024 * 1024
+            collective_id=0, has_side_effects=True, vmem_limit_bytes=60 * 1024 * 1024
         ),
     )(three_centre, block_mask, g_occ.T, g_virt)
 

time: 69.5 us -> 63.9 us (0.919)
  local copies, waits for them, and re-layouts: 5.43 us -> 1.47 us
  Pallas kernels: 63.8 us -> 62.2 us
    unnamed x9 -> x1, local copies, waits for them, and re-layouts: 5.43 us -> 1.47 us
    pallas_call x1, Pallas kernels: 63.8 us -> 62.2 us  [shards(): pl.pallas_call(body, out_shape=jax.ShapeDtypeStruct((NJ, NP, M), BF16), i...]
where the time goes in v3:
time: 63.9 us; the launch traced here: 63.7 us
  Pallas kernels  62.2 us (97%)
  local copies, waits for them, and re-layouts  1.47 us (2%)
    pallas_call x1, Pallas kernels, shards(): pl.pallas_call(body, out_shape=jax.ShapeDtypeStruct((NJ, NP, M), BF16), i...  62.2 us
    unnamed x1, local copies, waits for them, and re-layouts  1.47 us

profile of v3, /device:TPU:1, one launch (start us, length us, event | category | flops | bytes accessed | tf_op | source)
XLA Modules:
  0.0 63.7 jit_solution(8394311195933436436)
XLA Ops:
  0.0 62.2 %shard_map.46 = bf16[4,64,128]{2,1,0:T(8,128)(2,1)} custom-call(bf16[64,128,256]{2,1,0:T(8,128)(2,1)} %refs_0_.1, s32[1,2,4]{2,1,0:T(2,128)} %refs_1_.1, bf16[192,256]{1,0:T(8,128)(2,1)} %bitcast.1, bf16[128,2048]{1,0:T(8,128)(2,1)} %refs_3_.1), custom_call_target="tpu_custom_call" | custom-call | tf_op jit(solution)/shard_map/pallas_call | solution.py:520
  62.2 1.5 %copy.6 = bf16[4,64,128]{2,1,0:T(8,128)(2,1)} copy(bf16[4,64,128]{2,1,0:T(8,128)(2,1)} %shard_map.46) | data formatting | bytes 131072
